TPU v7x, 512 devices: a whole 4x8x8 slice. The times are simulated.
512 devices in a mesh: row: 8 (over z), col: 16 (over y, core), depth: 4 (over x).
Axes of the slice: x: 4, y: 8, z: 8, core: 2. Of those that a mesh axis runs over, the one named last changes fastest.
Arguments:
- tokens: bfloat16 [4096, 8192], P(('row', 'col'), 'depth'), may hold values from -6 to 6
- gate_weight: bfloat16 [8192, 14336], P(('depth', 'row'), 'col'), may hold values from -0.0625 to 0.0625
- up_weight: bfloat16 [8192, 14336], P(('depth', 'row'), 'col'), may hold values from -0.0625 to 0.0625
- down_weight: bfloat16 [14336, 8192], P(('col', 'row'), 'depth'), may hold values from -0.125 to 0.125
- gate_keep: int32 [64, 112], replicated, may hold values from 0 to 1, as said below
- up_keep: int32 [64, 112], replicated, may hold values from 0 to 1, as said below
- down_keep: int32 [112, 64], replicated, may hold values from 0 to 1, as said below
Outputs:
- mixed: bfloat16 [4096, 8192], P(('row', 'col'), 'depth')
Inputs may be any that keep to these rules, and one draw needn't show every extreme that they name: `gate_keep`: 1 marks a kept block of the gate projection, 0 a dropped one. `up_keep`: 1 marks a kept block of the up projection, 0 a dropped one. `down_keep`: 1 marks a kept block of the down projection, 0 a dropped one.
All inputs are finite; a program needn't handle non-finite values.
Results may differ from a plain program's by a relative error of at most 0.005.
Values may be sent and summed in bfloat16 or wider, within the bound.
No kernel may reach another device: no remote copies, remote signals or barrier semaphores. Data moves between devices by JAX's collectives and lax.ppermute only.
A program may use at most 64 MiB of HBM per device.

v0:
```python
import jax
import jax.numpy as jnp
from jax import lax
from jax.sharding import PartitionSpec as P

BLOCK = 128


def keep_table(keep, row_start, col_start, row_count, col_count):
    keep_bits = keep.astype(jnp.bfloat16)
    row_ids = (row_start + jnp.arange(row_count, dtype=jnp.int32)) // BLOCK
    col_ids = (col_start + jnp.arange(col_count, dtype=jnp.int32)) // BLOCK
    pick_rows = (row_ids[:, None] == jnp.arange(keep.shape[0], dtype=jnp.int32)[None, :]).astype(
        jnp.bfloat16
    )
    pick_cols = (jnp.arange(keep.shape[1], dtype=jnp.int32)[:, None] == col_ids[None, :]).astype(
        jnp.bfloat16
    )
    inner = jnp.dot(keep_bits, pick_cols, preferred_element_type=jnp.float32).astype(jnp.bfloat16)
    return jnp.dot(pick_rows, inner, preferred_element_type=jnp.float32).astype(jnp.bfloat16)


def add_panel(token_block, piece):
    return jnp.dot(token_block, piece, preferred_element_type=jnp.float32)


def on_device(tokens, gate_weight, up_weight, down_weight, gate_keep, up_keep, down_keep):
    depth_pos = lax.axis_index("depth")
    row_pos = lax.axis_index("row")
    column_pos = lax.axis_index("col")
    row_total = lax.axis_size("row")
    feature_rows = gate_weight.shape[0]
    hidden_cols = gate_weight.shape[1]
    feature_start = (depth_pos * row_total + row_pos) * feature_rows
    hidden_start = column_pos * hidden_cols
    gate_masked = gate_weight * keep_table(
        gate_keep, feature_start, hidden_start, feature_rows, hidden_cols
    )
    up_masked = up_weight * keep_table(
        up_keep, feature_start, hidden_start, feature_rows, hidden_cols
    )
    down_rows_count = down_weight.shape[0]
    down_features = down_weight.shape[1]
    down_start = (column_pos * row_total + row_pos) * down_rows_count
    down_masked = down_weight * keep_table(
        down_keep, down_start, depth_pos * down_features, down_rows_count, down_features
    )
    token_block = lax.all_gather(tokens, "col", axis=0, tiled=True)

    def add_one(piece):
        return add_panel(token_block, piece)

    gate = add_one(lax.all_gather(gate_masked, "row", axis=0, tiled=True))
    up = add_one(lax.all_gather(up_masked, "row", axis=0, tiled=True))
    both = jnp.stack((gate, up), 0)
    total = lax.psum(both, "depth")
    hidden = (jax.nn.silu(total[0]) * total[1]).astype(jnp.bfloat16)
    down_block = lax.all_gather(down_masked, "row", axis=0, tiled=True)
    mixed = lax.psum_scatter(
        jnp.dot(hidden, down_block, preferred_element_type=jnp.float32),
        "col",
        scatter_dimension=0,
        tiled=True,
    )
    return mixed.astype(jnp.bfloat16)


def solution(mesh):
    placed = (
        P(("row", "col"), "depth"),
        P(("depth", "row"), "col"),
        P(("depth", "row"), "col"),
        P(("col", "row"), "depth"),
        P(),
        P(),
        P(),
    )
    return jax.shard_map(
        on_device, mesh=mesh, in_specs=placed, out_specs=P(("row", "col"), "depth"), check_vma=False
    )
```

profile of v0, /device:TPU:25, one launch (start us, length us, event | category | flops | bytes accessed | tf_op | source)
XLA Modules:
  0.0 393.9 jit_solution(8674119538249657588)
XLA Ops:
  6.5 0.0 copy-start
  6.5 0.0 copy-start.1
  6.5 0.0 all-gather.7.cloned.1.call-start
  6.5 0.7 all-gather.7.cloned.1.call-update
  7.3 0.0 all-gather.9.cloned.1.call-start
  7.4 2.3 fusion.4
  9.7 0.0 all-gather.9.cloned.1.call-update
  9.7 0.0 all-gather.5.cloned.1.call-start
  9.8 2.3 fusion.3
  12.1 0.0 all-gather.5.cloned.1.call-update
  12.1 0.0 all-gather.11.cloned.1.call-start
  12.2 0.0 copy-done
  12.2 0.0 copy-done.1
  12.2 1.4 fusion
  13.7 0.0 all-gather.11.cloned.1.call-update
  13.7 0.0 all-reduce.2.cloned.1.call-start
  13.7 42.2 %all-gather.7.cloned.1.call-done = bf16[512,2048]{1,0:T(8,128)(2,1)} async-done(((bf16[32,2048]{1,0:T(8,128)(2,1)}), bf16[512,2048]{1,0:T(8,128)(2,1)}) %all-gather.7.cloned.1.call-update) | async-done | bytes 2097168 | tf_op jit(solution)/shard_map/all_gather | solution.py:48
  55.9 54.2 %all-gather.9.cloned.1.call-done = bf16[2048,896]{1,0:T(8,128)(2,1)} async-done(((bf16[256,896]{1,0:T(8,128)(2,1)}), bf16[2048,896]{1,0:T(8,128)(2,1)}) %all-gather.9.cloned.1.call-update) | async-done | bytes 3670032 | tf_op jit(solution)/shard_map/all_gather | solution.py:54
  110.2 4.8 %convolution_bitcast_fusion = f32[1,512,896]{1,2,0:T(8,128)S(1)} fusion(bf16[2048,896]{1,0:T(8,128)(2,1)} %all-gather.9.cloned.1.call-done, bf16[512,2048]{1,0:T(8,128)(2,1)} %all-gather.7.cloned.1.call-done), kind=kOutput, calls=%fused_computation.8 | convolution fusion | flops 1879048192 | bytes 7602176 | tf_op jit(solution)/shard_map/dot_general | solution.py:24
  115.0 48.7 %all-gather.5.cloned.1.call-done = bf16[2048,896]{1,0:T(8,128)(2,1)} async-done(((bf16[256,896]{1,0:T(8,128)(2,1)}), bf16[2048,896]{1,0:T(8,128)(2,1)}) %all-gather.5.cloned.1.call-update) | async-done | bytes 3670032 | tf_op jit(solution)/shard_map/all_gather | solution.py:53
  163.7 4.8 %convolution_bitcast_fusion.1 = f32[1,512,896]{1,2,0:T(8,128)S(1)} fusion(bf16[2048,896]{1,0:T(8,128)(2,1)} %all-gather.5.cloned.1.call-done, bf16[512,2048]{1,0:T(8,128)(2,1)} %all-gather.7.cloned.1.call-done), kind=kOutput, calls=%fused_computation.9 | convolution fusion | flops 1879048192 | bytes 7602176 | tf_op jit(solution)/shard_map/dot_general | solution.py:24
  168.5 2.3 pad_maximum_fusion
  170.8 0.0 all-reduce.2.cloned.1.call-update
  170.9 0.0 reduce-scatter.2.cloned.1.call-start
  170.9 46.2 %all-gather.11.cloned.1.call-done = bf16[896,2048]{1,0:T(8,128)(2,1)} async-done(((bf16[112,2048]{1,0:T(8,128)(2,1)}), bf16[896,2048]{1,0:T(8,128)(2,1)}) %all-gather.11.cloned.1.call-update) | async-done | bytes 3670032 | tf_op jit(solution)/shard_map/all_gather | solution.py:58
  217.1 95.3 %all-reduce.2.cloned.1.call-done = f32[2,512,896]{1,2,0:T(8,128)} async-done(((f32[2,512,896]{1,2,0:T(8,128)}), f32[2,512,896]{1,2,0:T(8,128)}) %all-reduce.2.cloned.1.call-update) | async-done | bytes 3670032 | tf_op jit(solution)/shard_map/psum | solution.py:56
  312.4 7.7 %fusion.5 = f32[512,2048]{1,0:T(8,128)} fusion(bf16[896,2048]{1,0:T(8,128)(2,1)} %all-gather.11.cloned.1.call-done, f32[2,512,896]{1,2,0:T(8,128)} %all-reduce.2.cloned.1.call-done), kind=kOutput, calls=%fused_computation.16 | convolution fusion | flops 1881800704 | bytes 11534336 | tf_op jit(solution)/shard_map/dot_general | solution.py:60
  320.0 0.0 reduce-scatter.2.cloned.1.call-update
  320.1 65.3 %reduce-scatter.2.cloned.1.call-done = f32[32,2048]{1,0:T(8,128)} async-done(((f32[512,2048]{1,0:T(8,128)}), f32[32,2048]{1,0:T(8,128)}) %reduce-scatter.2.cloned.1.call-update) | async-done | bytes 262160 | tf_op jit(solution)/shard_map/reduce_scatter | solution.py:59
  385.4 1.6 convert_element_type.52
  (4 shorter events, 0.0 us)
Async XLA Ops:
  6.5 5.7 %copy-start = (bf16[112,2048]{1,0:T(8,128)(2,1)S(1)}, bf16[112,2048]{1,0:T(8,128)(2,1)}, u32[]{:S(2)}) copy-start(bf16[112,2048]{1,0:T(8,128)(2,1)} %param.10) | copy-start | bytes 1376260
  6.5 5.7 %copy-start.1 = (s32[112,64]{0,1:T(8,128)S(1)}, s32[112,64]{0,1:T(8,128)}, u32[]{:S(2)}) copy-start(s32[112,64]{0,1:T(8,128)} %param.13) | copy-start | bytes 86020
  6.5 49.4 %all-gather.7.cloned.1.call-start = ((), (), s32[]{:S(2)}) async-start(), calls=%async_computation.2 | async-start | bytes 2228224 | tf_op jit(solution)/shard_map/all_gather | solution.py:48
  7.3 102.9 %all-gather.9.cloned.1.call-start = ((), (), s32[]{:S(2)}) async-start(), calls=%async_computation.3 | async-start | bytes 4128768 | tf_op jit(solution)/shard_map/all_gather | solution.py:54
  9.7 154.0 %all-gather.5.cloned.1.call-start = ((), (), s32[]{:S(2)}) async-start(), calls=%async_computation.1 | async-start | bytes 4128768 | tf_op jit(solution)/shard_map/all_gather | solution.py:53
  12.1 205.0 %all-gather.11.cloned.1.call-start = ((), (), s32[]{:S(2)}) async-start(), calls=%async_computation.5 | async-start | bytes 4128768 | tf_op jit(solution)/shard_map/all_gather | solution.py:58
  13.7 298.7 %all-reduce.2.cloned.1.call-start = ((), (), s32[]{:S(2)}) async-start(), calls=%async_computation.4 | async-start | bytes 7340032 | tf_op jit(solution)/shard_map/psum | solution.py:56
  170.9 214.5 %reduce-scatter.2.cloned.1.call-start = ((), (), s32[]{:S(2)}) async-start(), calls=%async_computation.6 | async-start | bytes 4456448 | tf_op jit(solution)/shard_map/reduce_scatter | solution.py:59
Sparse Core Ops, SparseCore 0:
  9.5 46.3 all-gather.6
  58.0 52.1 all-gather.8
  112.2 51.4 all-gather.4
  165.6 51.3 all-gather.10
  219.3 93.0 all-reduce.1
  320.2 65.1 reduce-scatter.1
where the time goes:
time: 394 us
  waiting for transfers between devices  353 us (90%)
  matrix products  23.4 us (6%)
  between operations  13.5 us (3%)
  other arithmetic  4 us (1%)
    psum x1, waiting for transfers between devices, on_device(): total = lax.psum(both, 'depth')  95.3 us
    reduce_scatter x1, waiting for transfers between devices, on_device(): lax.psum_scatter(jnp.dot(hidden, down_block, preferred_element_type=jnp.f...  65.3 us
    all_gather x1, waiting for transfers between devices, on_device(): up = add_one(lax.all_gather(up_masked, 'row', axis=0, tiled=True))  54.2 us
    all_gather x1, waiting for transfers between devices, on_device(): gate = add_one(lax.all_gather(gate_masked, 'row', axis=0, tiled=True))  48.7 us
    all_gather x1, waiting for transfers between devices, on_device(): down_block = lax.all_gather(down_masked, 'row', axis=0, tiled=True)  46.2 us
    all_gather x1, waiting for transfers between devices, on_device(): token_block = lax.all_gather(tokens, 'col', axis=0, tiled=True)  42.2 us
    dot_general x2, matrix products, add_panel(): return jnp.dot(token_block, piece, preferred_element_type=jnp.float32)  9.61 us
  transfers between devices with their start and end apart: 6, of which 6 were waited for; matrix products, arithmetic and copies ran while one was open for 5% of the time, Pallas kernels for 0%

commit v1 on v0

--- a/solution.py
+++ b/solution.py
@@ -45,7 +45,12 @@
     down_masked = down_weight * keep_table(
         down_keep, down_start, depth_pos * down_features, down_rows_count, down_features
     )
-    token_block = lax.all_gather(tokens, "col", axis=0, tiled=True)
+    ring = [tokens]
+    for hop in range(15):
+        ring.append(lax.ppermute(ring[-1], "col", [(dev, (dev + 1) % 16) for dev in range(16)]))
+    token_block = jnp.roll(
+        jnp.concatenate(ring[::-1], axis=0), (lax.axis_index("col") + 1) * ring[0].shape[0], axis=0
+    )
 
     def add_one(piece):
         return add_panel(token_block, piece)

time: 394 us -> 351 us (0.89)
  waiting for transfers between devices: 353 us -> 234 us
  starting transfers between devices: 0.21 us -> 54.3 us
  local copies, waits for them, and re-layouts: 0.01 us -> 21 us
    all_gather x1, waiting for transfers between devices: 54.2 us -> 0.02 us  [on_device(): up = add_one(lax.all_gather(up_masked, 'row', axis=0, tiled=True))]
    ppermute x0 -> x15, starting transfers between devices: none -> 54.1 us  [on_device(): lax.ppermute(ring[-1], 'col', [(dev, (dev + 1) % 16) for dev in range(16)])]
    all_gather x1, waiting for transfers between devices: 48.7 us -> 0.01 us  [on_device(): gate = add_one(lax.all_gather(gate_masked, 'row', axis=0, tiled=True))]
    all_gather x1 -> x0, waiting for transfers between devices: 42.2 us -> none  [on_device(): token_block = lax.all_gather(tokens, 'col', axis=0, tiled=True)]
    ppermute x0 -> x15, waiting for transfers between devices: none -> 27.6 us  [on_device(): lax.ppermute(ring[-1], 'col', [(dev, (dev + 1) % 16) for dev in range(16)])]
    unnamed x4 -> x33, local copies, waits for them, and re-layouts: 0.01 us -> 20.4 us
  transfers between devices with their start and end apart: 6 -> 20, of which waited for: 6 -> 17; matrix products, arithmetic and copies ran while one was open for 5% -> 11% of each run, Pallas kernels for 0% -> 0%
where the time goes in v1:
time: 351 us
  waiting for transfers between devices  234 us (67%)
  starting transfers between devices  54.3 us (15%)
  matrix products  24.7 us (7%)
  local copies, waits for them, and re-layouts  21 us (6%)
  between operations  13.2 us (4%)
  other arithmetic  3.68 us (1%)
    psum x1, waiting for transfers between devices, on_device(): total = lax.psum(both, 'depth')  95.3 us
    reduce_scatter x1, waiting for transfers between devices, on_device(): lax.psum_scatter(jnp.dot(hidden, down_block, preferred_element_type=jnp.f...  65.4 us
    ppermute x15, starting transfers between devices, on_device(): lax.ppermute(ring[-1], 'col', [(dev, (dev + 1) % 16) for dev in range(16)])  54.1 us
    all_gather x1, waiting for transfers between devices, on_device(): down_block = lax.all_gather(down_masked, 'row', axis=0, tiled=True)  45.3 us
    ppermute x15, waiting for transfers between devices, on_device(): lax.ppermute(ring[-1], 'col', [(dev, (dev + 1) % 16) for dev in range(16)])  27.6 us
    unnamed x33, local copies, waits for them, and re-layouts  20.4 us
    dot_general x2, matrix products, add_panel(): return jnp.dot(token_block, piece, preferred_element_type=jnp.float32)  9.99 us
    dot_general x1, matrix products, on_device(): jnp.dot(hidden, down_block, preferred_element_type=jnp.float32)  7.46 us
  transfers between devices with their start and end apart: 20, of which 17 were waited for; matrix products, arithmetic and copies ran while one was open for 11% of the time, Pallas kernels for 0%

profile of v1, /device:TPU:25, one launch (start us, length us, event | category | flops | bytes accessed | tf_op | source)
XLA Modules:
  0.0 350.6 jit_solution(2601957791248896709)
XLA Ops:
  6.6 2.4 fusion.13
  9.0 2.4 fusion.14
  11.5 3.1 collective-permute-start
  14.5 2.3 collective-permute-done
  16.8 3.5 %collective-permute-start.1 = (bf16[32,2048]{1,0:T(8,128)(2,1)S(1)}, bf16[32,2048]{1,0:T(8,128)(2,1)S(1)}, u32[]{:S(2)}, u32[]{:S(2)}) collective-permute-start(bf16[32,2048]{1,0:T(8,128)(2,1)S(1)} %collective-permute-done), channel_id=1, source_target_pairs={{0,4},{4,8},{8,12},{12,16},{16,20},{20,24},{24,28},{28,32},{32,36}... | collective-permute-start | bytes 393224 | tf_op jit(solution)/shard_map/ppermute | solution.py:50
  20.4 1.9 collective-permute-done.1
  22.3 3.7 %collective-permute-start.2 = (bf16[32,2048]{1,0:T(8,128)(2,1)S(1)}, bf16[32,2048]{1,0:T(8,128)(2,1)S(1)}, u32[]{:S(2)}, u32[]{:S(2)}) collective-permute-start(bf16[32,2048]{1,0:T(8,128)(2,1)S(1)} %collective-permute-done.1), channel_id=1, source_target_pairs={{0,4},{4,8},{8,12},{12,16},{16,20},{20,24},{24,28},{28,32},{32,36}... | collective-permute-start | bytes 393224 | tf_op jit(solution)/shard_map/ppermute | solution.py:50
  26.0 1.9 collective-permute-done.2
  27.9 3.7 %collective-permute-start.3 = (bf16[32,2048]{1,0:T(8,128)(2,1)S(1)}, bf16[32,2048]{1,0:T(8,128)(2,1)S(1)}, u32[]{:S(2)}, u32[]{:S(2)}) collective-permute-start(bf16[32,2048]{1,0:T(8,128)(2,1)S(1)} %collective-permute-done.2), channel_id=1, source_target_pairs={{0,4},{4,8},{8,12},{12,16},{16,20},{20,24},{24,28},{28,32},{32,36}... | collective-permute-start | bytes 393224 | tf_op jit(solution)/shard_map/ppermute | solution.py:50
  31.6 1.9 collective-permute-done.3
  33.5 3.7 %collective-permute-start.4 = (bf16[32,2048]{1,0:T(8,128)(2,1)S(1)}, bf16[32,2048]{1,0:T(8,128)(2,1)S(1)}, u32[]{:S(2)}, u32[]{:S(2)}) collective-permute-start(bf16[32,2048]{1,0:T(8,128)(2,1)S(1)} %collective-permute-done.3), channel_id=1, source_target_pairs={{0,4},{4,8},{8,12},{12,16},{16,20},{20,24},{24,28},{28,32},{32,36}... | collective-permute-start | bytes 393224 | tf_op jit(solution)/shard_map/ppermute | solution.py:50
  37.2 1.9 collective-permute-done.4
  39.1 3.7 %collective-permute-start.5 = (bf16[32,2048]{1,0:T(8,128)(2,1)S(1)}, bf16[32,2048]{1,0:T(8,128)(2,1)S(1)}, u32[]{:S(2)}, u32[]{:S(2)}) collective-permute-start(bf16[32,2048]{1,0:T(8,128)(2,1)S(1)} %collective-permute-done.4), channel_id=1, source_target_pairs={{0,4},{4,8},{8,12},{12,16},{16,20},{20,24},{24,28},{28,32},{32,36}... | collective-permute-start | bytes 393224 | tf_op jit(solution)/shard_map/ppermute | solution.py:50
  44.7 3.7 %collective-permute-start.6 = (bf16[32,2048]{1,0:T(8,128)(2,1)S(1)}, bf16[32,2048]{1,0:T(8,128)(2,1)S(1)}, u32[]{:S(2)}, u32[]{:S(2)}) collective-permute-start(bf16[32,2048]{1,0:T(8,128)(2,1)S(1)} %collective-permute-done.5), channel_id=1, source_target_pairs={{0,4},{4,8},{8,12},{12,16},{16,20},{20,24},{24,28},{28,32},{32,36}... | collective-permute-start | bytes 393224 | tf_op jit(solution)/shard_map/ppermute | solution.py:50
  48.4 1.9 collective-permute-done.6
  50.3 3.7 %collective-permute-start.7 = (bf16[32,2048]{1,0:T(8,128)(2,1)S(1)}, bf16[32,2048]{1,0:T(8,128)(2,1)S(1)}, u32[]{:S(2)}, u32[]{:S(2)}) collective-permute-start(bf16[32,2048]{1,0:T(8,128)(2,1)S(1)} %collective-permute-done.6), channel_id=1, source_target_pairs={{0,4},{4,8},{8,12},{12,16},{16,20},{20,24},{24,28},{28,32},{32,36}... | collective-permute-start | bytes 393224 | tf_op jit(solution)/shard_map/ppermute | solution.py:50
  55.9 3.7 %collective-permute-start.8 = (bf16[32,2048]{1,0:T(8,128)(2,1)S(1)}, bf16[32,2048]{1,0:T(8,128)(2,1)S(1)}, u32[]{:S(2)}, u32[]{:S(2)}) collective-permute-start(bf16[32,2048]{1,0:T(8,128)(2,1)S(1)} %collective-permute-done.7), channel_id=1, source_target_pairs={{0,4},{4,8},{8,12},{12,16},{16,20},{20,24},{24,28},{28,32},{32,36}... | collective-permute-start | bytes 393224 | tf_op jit(solution)/shard_map/ppermute | solution.py:50
  59.6 1.9 collective-permute-done.8
  61.5 3.7 %collective-permute-start.9 = (bf16[32,2048]{1,0:T(8,128)(2,1)S(1)}, bf16[32,2048]{1,0:T(8,128)(2,1)S(1)}, u32[]{:S(2)}, u32[]{:S(2)}) collective-permute-start(bf16[32,2048]{1,0:T(8,128)(2,1)S(1)} %collective-permute-done.8), channel_id=1, source_target_pairs={{0,4},{4,8},{8,12},{12,16},{16,20},{20,24},{24,28},{28,32},{32,36}... | collective-permute-start | bytes 393224 | tf_op jit(solution)/shard_map/ppermute | solution.py:50
  67.1 3.7 %collective-permute-start.10 = (bf16[32,2048]{1,0:T(8,128)(2,1)S(1)}, bf16[32,2048]{1,0:T(8,128)(2,1)S(1)}, u32[]{:S(2)}, u32[]{:S(2)}) collective-permute-start(bf16[32,2048]{1,0:T(8,128)(2,1)S(1)} %collective-permute-done.9), channel_id=1, source_target_pairs={{0,4},{4,8},{8,12},{12,16},{16,20},{20,24},{24,28},{28,32},{32,36}... | collective-permute-start | bytes 393224 | tf_op jit(solution)/shard_map/ppermute | solution.py:50
  72.7 3.7 %collective-permute-start.11 = (bf16[32,2048]{1,0:T(8,128)(2,1)S(1)}, bf16[32,2048]{1,0:T(8,128)(2,1)S(1)}, u32[]{:S(2)}, u32[]{:S(2)}) collective-permute-start(bf16[32,2048]{1,0:T(8,128)(2,1)S(1)} %collective-permute-done.10), channel_id=1, source_target_pairs={{0,4},{4,8},{8,12},{12,16},{16,20},{20,24},{24,28},{28,32},{32,36}... | collective-permute-start | bytes 393224 | tf_op jit(solution)/shard_map/ppermute | solution.py:50
  78.3 3.7 %collective-permute-start.12 = (bf16[32,2048]{1,0:T(8,128)(2,1)S(1)}, bf16[32,2048]{1,0:T(8,128)(2,1)S(1)}, u32[]{:S(2)}, u32[]{:S(2)}) collective-permute-start(bf16[32,2048]{1,0:T(8,128)(2,1)S(1)} %collective-permute-done.11), channel_id=1, source_target_pairs={{0,4},{4,8},{8,12},{12,16},{16,20},{20,24},{24,28},{28,32},{32,36}... | collective-permute-start | bytes 393224 | tf_op jit(solution)/shard_map/ppermute | solution.py:50
  83.9 3.7 %collective-permute-start.13 = (bf16[32,2048]{1,0:T(8,128)(2,1)S(1)}, bf16[32,2048]{1,0:T(8,128)(2,1)S(1)}, u32[]{:S(2)}, u32[]{:S(2)}) collective-permute-start(bf16[32,2048]{1,0:T(8,128)(2,1)S(1)} %collective-permute-done.12), channel_id=1, source_target_pairs={{0,4},{4,8},{8,12},{12,16},{16,20},{20,24},{24,28},{28,32},{32,36}... | collective-permute-start | bytes 393224 | tf_op jit(solution)/shard_map/ppermute | solution.py:50
  89.6 3.7 %collective-permute-start.14 = (bf16[32,2048]{1,0:T(8,128)(2,1)S(1)}, bf16[32,2048]{1,0:T(8,128)(2,1)S(1)}, u32[]{:S(2)}, u32[]{:S(2)}) collective-permute-start(bf16[32,2048]{1,0:T(8,128)(2,1)S(1)} %collective-permute-done.13), channel_id=1, source_target_pairs={{0,4},{4,8},{8,12},{12,16},{16,20},{20,24},{24,28},{28,32},{32,36}... | collective-permute-start | bytes 393224 | tf_op jit(solution)/shard_map/ppermute | solution.py:50
  93.2 2.5 fusion
  116.9 5.0 %fusion.7 = f32[1,512,896]{2,1,0:T(8,128)S(1)} fusion(bf16[2048,896]{1,0:T(8,128)(2,1)} %all-gather.4.cloned.1.call-done, bf16[1024,2048]{1,0:T(8,128)(2,1)} %constant_dynamic-update-slice_fusion, s32[]{:T(128)S(6)} %select_n.52), kind=kOutput, calls=%fused_computation.12 | convolution fusion | flops 1879048192 | bytes 7602180 | tf_op jit(solution)/shard_map/dot_general | solution.py:24
  121.9 5.0 %fusion.10 = f32[1,512,896]{2,1,0:T(8,128)S(1)} fusion(bf16[2048,896]{1,0:T(8,128)(2,1)} %all-gather.6.cloned.1.call-done, bf16[1024,2048]{1,0:T(8,128)(2,1)} %constant_dynamic-update-slice_fusion, s32[]{:T(128)S(6)} %select_n.52), kind=kOutput, calls=%fused_computation.13 | convolution fusion | flops 1879048192 | bytes 7602180 | tf_op jit(solution)/shard_map/dot_general | solution.py:24
  126.9 2.0 pad_maximum_fusion
  129.0 45.3 %all-gather.8.cloned.1.call-done = bf16[896,2048]{1,0:T(8,128)(2,1)} async-done(((bf16[112,2048]{1,0:T(8,128)(2,1)}), bf16[896,2048]{1,0:T(8,128)(2,1)}) %all-gather.8.cloned.1.call-update) | async-done | bytes 3670032 | tf_op jit(solution)/shard_map/all_gather | solution.py:63
  174.2 95.3 %all-reduce.2.cloned.1.call-done = f32[2,512,896]{2,1,0:T(8,128)} async-done(((f32[2,512,896]{2,1,0:T(8,128)}), f32[2,512,896]{2,1,0:T(8,128)}) %all-reduce.2.cloned.1.call-update) | async-done | bytes 3670032 | tf_op jit(solution)/shard_map/psum | solution.py:61
  269.6 7.5 %fusion.15 = f32[512,2048]{1,0:T(8,128)} fusion(bf16[896,2048]{1,0:T(8,128)(2,1)} %all-gather.8.cloned.1.call-done, f32[2,512,896]{2,1,0:T(8,128)} %all-reduce.2.cloned.1.call-done), kind=kOutput, calls=%fused_computation.20 | convolution fusion | flops 1881800704 | bytes 11534336 | tf_op jit(solution)/shard_map/dot_general | solution.py:65
  277.0 65.4 %reduce-scatter.2.cloned.1.call-done = f32[32,2048]{1,0:T(8,128)} async-done(((f32[512,2048]{1,0:T(8,128)}), f32[32,2048]{1,0:T(8,128)}) %reduce-scatter.2.cloned.1.call-update) | async-done | bytes 262160 | tf_op jit(solution)/shard_map/reduce_scatter | solution.py:64
  (59 shorter events, 36.6 us)
Async XLA Ops:
  6.5 99.2 %copy-start = (bf16[32,2048]{1,0:T(8,128)(2,1)S(1)}, bf16[32,2048]{1,0:T(8,128)(2,1)}, u32[]{:S(2)}) copy-start(bf16[32,2048]{1,0:T(8,128)(2,1)} %param.7) | copy-start | bytes 393220
  6.5 110.3 %all-gather.4.cloned.1.call-start = ((), (), s32[]{:S(2)}) async-start(), calls=%async_computation.1 | async-start | bytes 4128768 | tf_op jit(solution)/shard_map/all_gather | solution.py:58
  9.0 112.9 %all-gather.6.cloned.1.call-start = ((), (), s32[]{:S(2)}) async-start(), calls=%async_computation.2 | async-start | bytes 4128768 | tf_op jit(solution)/shard_map/all_gather | solution.py:59
  11.4 162.8 %all-gather.8.cloned.1.call-start = ((), (), s32[]{:S(2)}) async-start(), calls=%async_computation.4 | async-start | bytes 4128768 | tf_op jit(solution)/shard_map/all_gather | solution.py:63
  11.5 5.3 %collective-permute-start = (bf16[32,2048]{1,0:T(8,128)(2,1)}, bf16[32,2048]{1,0:T(8,128)(2,1)S(1)}, u32[]{:S(2)}, u32[]{:S(2)}) collective-permute-start(bf16[32,2048]{1,0:T(8,128)(2,1)} %param.7), channel_id=1, source_target_pairs={{0,4},{4,8},{8,12},{12,16},{16,20},{20,24},{24,28},{28,32},{32,36}... | collective-permute-start | bytes 393224 | tf_op jit(solution)/shard_map/ppermute | solution.py:50
  16.8 5.5 %collective-permute-start.1 = (bf16[32,2048]{1,0:T(8,128)(2,1)S(1)}, bf16[32,2048]{1,0:T(8,128)(2,1)S(1)}, u32[]{:S(2)}, u32[]{:S(2)}) collective-permute-start(bf16[32,2048]{1,0:T(8,128)(2,1)S(1)} %collective-permute-done), channel_id=1, source_target_pairs={{0,4},{4,8},{8,12},{12,16},{16,20},{20,24},{24,28},{28,32},{32,36}... | collective-permute-start | bytes 393224 | tf_op jit(solution)/shard_map/ppermute | solution.py:50
  22.3 5.6 %collective-permute-start.2 = (bf16[32,2048]{1,0:T(8,128)(2,1)S(1)}, bf16[32,2048]{1,0:T(8,128)(2,1)S(1)}, u32[]{:S(2)}, u32[]{:S(2)}) collective-permute-start(bf16[32,2048]{1,0:T(8,128)(2,1)S(1)} %collective-permute-done.1), channel_id=1, source_target_pairs={{0,4},{4,8},{8,12},{12,16},{16,20},{20,24},{24,28},{28,32},{32,36}... | collective-permute-start | bytes 393224 | tf_op jit(solution)/shard_map/ppermute | solution.py:50
  27.9 5.6 %collective-permute-start.3 = (bf16[32,2048]{1,0:T(8,128)(2,1)S(1)}, bf16[32,2048]{1,0:T(8,128)(2,1)S(1)}, u32[]{:S(2)}, u32[]{:S(2)}) collective-permute-start(bf16[32,2048]{1,0:T(8,128)(2,1)S(1)} %collective-permute-done.2), channel_id=1, source_target_pairs={{0,4},{4,8},{8,12},{12,16},{16,20},{20,24},{24,28},{28,32},{32,36}... | collective-permute-start | bytes 393224 | tf_op jit(solution)/shard_map/ppermute | solution.py:50
  33.5 5.6 %collective-permute-start.4 = (bf16[32,2048]{1,0:T(8,128)(2,1)S(1)}, bf16[32,2048]{1,0:T(8,128)(2,1)S(1)}, u32[]{:S(2)}, u32[]{:S(2)}) collective-permute-start(bf16[32,2048]{1,0:T(8,128)(2,1)S(1)} %collective-permute-done.3), channel_id=1, source_target_pairs={{0,4},{4,8},{8,12},{12,16},{16,20},{20,24},{24,28},{28,32},{32,36}... | collective-permute-start | bytes 393224 | tf_op jit(solution)/shard_map/ppermute | solution.py:50
  39.1 5.6 %collective-permute-start.5 = (bf16[32,2048]{1,0:T(8,128)(2,1)S(1)}, bf16[32,2048]{1,0:T(8,128)(2,1)S(1)}, u32[]{:S(2)}, u32[]{:S(2)}) collective-permute-start(bf16[32,2048]{1,0:T(8,128)(2,1)S(1)} %collective-permute-done.4), channel_id=1, source_target_pairs={{0,4},{4,8},{8,12},{12,16},{16,20},{20,24},{24,28},{28,32},{32,36}... | collective-permute-start | bytes 393224 | tf_op jit(solution)/shard_map/ppermute | solution.py:50
  44.7 5.6 %collective-permute-start.6 = (bf16[32,2048]{1,0:T(8,128)(2,1)S(1)}, bf16[32,2048]{1,0:T(8,128)(2,1)S(1)}, u32[]{:S(2)}, u32[]{:S(2)}) collective-permute-start(bf16[32,2048]{1,0:T(8,128)(2,1)S(1)} %collective-permute-done.5), channel_id=1, source_target_pairs={{0,4},{4,8},{8,12},{12,16},{16,20},{20,24},{24,28},{28,32},{32,36}... | collective-permute-start | bytes 393224 | tf_op jit(solution)/shard_map/ppermute | solution.py:50
  50.3 5.6 %collective-permute-start.7 = (bf16[32,2048]{1,0:T(8,128)(2,1)S(1)}, bf16[32,2048]{1,0:T(8,128)(2,1)S(1)}, u32[]{:S(2)}, u32[]{:S(2)}) collective-permute-start(bf16[32,2048]{1,0:T(8,128)(2,1)S(1)} %collective-permute-done.6), channel_id=1, source_target_pairs={{0,4},{4,8},{8,12},{12,16},{16,20},{20,24},{24,28},{28,32},{32,36}... | collective-permute-start | bytes 393224 | tf_op jit(solution)/shard_map/ppermute | solution.py:50
  55.9 5.6 %collective-permute-start.8 = (bf16[32,2048]{1,0:T(8,128)(2,1)S(1)}, bf16[32,2048]{1,0:T(8,128)(2,1)S(1)}, u32[]{:S(2)}, u32[]{:S(2)}) collective-permute-start(bf16[32,2048]{1,0:T(8,128)(2,1)S(1)} %collective-permute-done.7), channel_id=1, source_target_pairs={{0,4},{4,8},{8,12},{12,16},{16,20},{20,24},{24,28},{28,32},{32,36}... | collective-permute-start | bytes 393224 | tf_op jit(solution)/shard_map/ppermute | solution.py:50
  61.5 5.6 %collective-permute-start.9 = (bf16[32,2048]{1,0:T(8,128)(2,1)S(1)}, bf16[32,2048]{1,0:T(8,128)(2,1)S(1)}, u32[]{:S(2)}, u32[]{:S(2)}) collective-permute-start(bf16[32,2048]{1,0:T(8,128)(2,1)S(1)} %collective-permute-done.8), channel_id=1, source_target_pairs={{0,4},{4,8},{8,12},{12,16},{16,20},{20,24},{24,28},{28,32},{32,36}... | collective-permute-start | bytes 393224 | tf_op jit(solution)/shard_map/ppermute | solution.py:50
  67.1 5.6 %collective-permute-start.10 = (bf16[32,2048]{1,0:T(8,128)(2,1)S(1)}, bf16[32,2048]{1,0:T(8,128)(2,1)S(1)}, u32[]{:S(2)}, u32[]{:S(2)}) collective-permute-start(bf16[32,2048]{1,0:T(8,128)(2,1)S(1)} %collective-permute-done.9), channel_id=1, source_target_pairs={{0,4},{4,8},{8,12},{12,16},{16,20},{20,24},{24,28},{28,32},{32,36}... | collective-permute-start | bytes 393224 | tf_op jit(solution)/shard_map/ppermute | solution.py:50
  72.7 5.6 %collective-permute-start.11 = (bf16[32,2048]{1,0:T(8,128)(2,1)S(1)}, bf16[32,2048]{1,0:T(8,128)(2,1)S(1)}, u32[]{:S(2)}, u32[]{:S(2)}) collective-permute-start(bf16[32,2048]{1,0:T(8,128)(2,1)S(1)} %collective-permute-done.10), channel_id=1, source_target_pairs={{0,4},{4,8},{8,12},{12,16},{16,20},{20,24},{24,28},{28,32},{32,36}... | collective-permute-start | bytes 393224 | tf_op jit(solution)/shard_map/ppermute | solution.py:50
  78.3 5.6 %collective-permute-start.12 = (bf16[32,2048]{1,0:T(8,128)(2,1)S(1)}, bf16[32,2048]{1,0:T(8,128)(2,1)S(1)}, u32[]{:S(2)}, u32[]{:S(2)}) collective-permute-start(bf16[32,2048]{1,0:T(8,128)(2,1)S(1)} %collective-permute-done.11), channel_id=1, source_target_pairs={{0,4},{4,8},{8,12},{12,16},{16,20},{20,24},{24,28},{28,32},{32,36}... | collective-permute-start | bytes 393224 | tf_op jit(solution)/shard_map/ppermute | solution.py:50
  83.9 5.6 %collective-permute-start.13 = (bf16[32,2048]{1,0:T(8,128)(2,1)S(1)}, bf16[32,2048]{1,0:T(8,128)(2,1)S(1)}, u32[]{:S(2)}, u32[]{:S(2)}) collective-permute-start(bf16[32,2048]{1,0:T(8,128)(2,1)S(1)} %collective-permute-done.12), channel_id=1, source_target_pairs={{0,4},{4,8},{8,12},{12,16},{16,20},{20,24},{24,28},{28,32},{32,36}... | collective-permute-start | bytes 393224 | tf_op jit(solution)/shard_map/ppermute | solution.py:50
  89.6 6.2 %collective-permute-start.14 = (bf16[32,2048]{1,0:T(8,128)(2,1)S(1)}, bf16[32,2048]{1,0:T(8,128)(2,1)S(1)}, u32[]{:S(2)}, u32[]{:S(2)}) collective-permute-start(bf16[32,2048]{1,0:T(8,128)(2,1)S(1)} %collective-permute-done.13), channel_id=1, source_target_pairs={{0,4},{4,8},{8,12},{12,16},{16,20},{20,24},{24,28},{28,32},{32,36}... | collective-permute-start | bytes 393224 | tf_op jit(solution)/shard_map/ppermute | solution.py:50
  95.7 173.8 %all-reduce.2.cloned.1.call-start = ((), (), s32[]{:S(2)}) async-start(), calls=%async_computation.3 | async-start | bytes 7340032 | tf_op jit(solution)/shard_map/psum | solution.py:61
  128.9 213.5 %reduce-scatter.2.cloned.1.call-start = ((), (), s32[]{:S(2)}) async-start(), calls=%async_computation.5 | async-start | bytes 4456448 | tf_op jit(solution)/shard_map/reduce_scatter | solution.py:64
Sparse Core Ops, SparseCore 0:
  9.4 57.7 all-gather.3
  69.3 51.3 all-gather.5
  122.8 51.3 all-gather.7
  176.5 93.0 all-reduce.1
  277.2 65.1 reduce-scatter.1
